TPU v7x, 512 devices: a whole 4x8x8 slice. The times are simulated.
512 devices in a mesh: dp: 32 (over x, y), seq: 16 (over z, core).
Axes of the slice: x: 4, y: 8, z: 8, core: 2. Of those that a mesh axis runs over, the one named last changes fastest.
Arguments:
- volume: bfloat16 [32, 3072, 1024], P('dp', 'seq')
- cotangent: bfloat16 [32, 3072, 1024], P('dp', 'seq'), may hold values from -6 to 6
- weights: bfloat16 [1024, 3, 1024], P('dp')
- pairs: int32 [32, 16, 24, 4], P('dp', 'seq'), may hold values from 0 to 23, as said below
- valid: int32 [32, 16, 24, 4], P('dp', 'seq'), may hold values from 0 to 1, as said below
Outputs:
- attended: bfloat16 [32, 3072, 1024], P('dp', 'seq')
- weight_grad: float32 [1024, 3, 1024], P('dp', None, 'seq')
Inputs may be any that keep to these rules, and one draw needn't show every extreme that they name: `pairs`: slot 0 of query block b holds b; the key blocks of one query block's slots are distinct. `valid`: slot 0 is always 1.
All inputs are finite; a program needn't handle non-finite values.
Results may differ from a plain program's by a relative error of at most 0.03.
Values may be sent and summed in bfloat16 or wider, within the bound.
No kernel may reach another device: no remote copies, remote signals or barrier semaphores. Data moves between devices by JAX's collectives and lax.ppermute only.
A program may use at most 64 MiB of HBM per device.

v0:
```python
import math
import jax
import jax.numpy as jnp
from jax import lax
from jax.sharding import PartitionSpec as P

HD = 64


def head_pass(queries, keys_all, values_all, upstream, pair_list, pair_live):
    block_count, slot_count = pair_list.shape
    all_rows, head_size = queries.shape
    block_rows = all_rows // block_count
    per_step = math.gcd(block_count, max(1, 512 // block_rows))
    steps_n = block_count // per_step
    scaling = head_size ** (-0.5)
    key_blocks = keys_all.reshape(block_count, block_rows, head_size)
    value_blocks = values_all.reshape(block_count, block_rows, head_size)
    block_index = jnp.arange(block_count, dtype=jnp.int32)

    def step(totals, sliced):
        key_total, value_total = totals
        query_rows, grad_rows, slot_blocks, slot_live = sliced
        key_rows = key_blocks[slot_blocks].reshape(per_step, slot_count * block_rows, head_size)
        value_rows = value_blocks[slot_blocks].reshape(per_step, slot_count * block_rows, head_size)
        live_cols = jnp.repeat(slot_live > 0, block_rows, axis=1)[:, None, :]
        scores = (
            jnp.einsum("nqd,nkd->nqk", query_rows, key_rows, preferred_element_type=jnp.float32)
            * scaling
        )
        row_max = jnp.max(jnp.where(live_cols, scores, -1e30), axis=-1, keepdims=True)
        exponent = jnp.where(live_cols, jnp.exp(scores - row_max), 0.0)
        prob_full = exponent / jnp.sum(exponent, axis=-1, keepdims=True)
        rounded = prob_full.astype(jnp.bfloat16)
        result = jnp.einsum(
            "nqk,nkd->nqd", rounded, value_rows, preferred_element_type=jnp.float32
        ).astype(jnp.bfloat16)
        value_grad = jnp.einsum(
            "nqk,nqd->nkd", rounded, grad_rows, preferred_element_type=jnp.float32
        )
        prob_grad = jnp.einsum(
            "nqd,nkd->nqk", grad_rows, value_rows, preferred_element_type=jnp.float32
        )
        row_dot = jnp.sum(
            grad_rows.astype(jnp.float32) * result.astype(jnp.float32), axis=-1, keepdims=True
        )
        score_grad = (prob_full * (prob_grad - row_dot) * scaling).astype(jnp.bfloat16)
        query_grad = jnp.einsum(
            "nqk,nkd->nqd", score_grad, key_rows, preferred_element_type=jnp.float32
        ).astype(jnp.bfloat16)
        key_grad = jnp.einsum(
            "nqk,nqd->nkd", score_grad, query_rows, preferred_element_type=jnp.float32
        )
        one_hot = (
            (slot_blocks.reshape(-1)[:, None] == block_index[None, :])
            & (slot_live.reshape(-1)[:, None] > 0)
        ).astype(jnp.float32)
        key_total = key_total + jnp.einsum(
            "jb,jrd->brd",
            one_hot,
            key_grad.reshape(per_step * slot_count, block_rows, head_size),
            precision=lax.Precision.HIGHEST,
        )
        value_total = value_total + jnp.einsum(
            "jb,jrd->brd",
            one_hot,
            value_grad.reshape(per_step * slot_count, block_rows, head_size),
            precision=lax.Precision.HIGHEST,
        )
        return ((key_total, value_total), (result, query_grad))

    empty_acc = jnp.zeros((block_count, block_rows, head_size), jnp.float32)
    sliced_all = (
        queries.reshape(steps_n, per_step, block_rows, head_size),
        upstream.reshape(steps_n, per_step, block_rows, head_size),
        pair_list.reshape(steps_n, per_step, slot_count),
        pair_live.reshape(steps_n, per_step, slot_count),
    )
    (key_total, value_total), (results, query_grads) = lax.scan(
        step, (empty_acc, empty_acc), sliced_all
    )
    return (
        results.reshape(all_rows, head_size),
        query_grads.reshape(all_rows, head_size),
        key_total.astype(jnp.bfloat16).reshape(all_rows, head_size),
        value_total.astype(jnp.bfloat16).reshape(all_rows, head_size),
    )


def local(volume, cotangent, weights, pairs, valid):
    seq_devices = lax.axis_size("seq")
    local_volume = volume[0]
    local_grad = cotangent[0]
    tok_count = local_volume.shape[0]
    width_all = local_grad.shape[1]
    local_cols = width_all // seq_devices
    all_rows = tok_count * seq_devices
    projected = jnp.einsum(
        "td,djc->tjc",
        local_volume,
        lax.all_gather(weights, "dp", axis=0, tiled=True),
        preferred_element_type=jnp.float32,
    )
    projected = projected.astype(jnp.bfloat16)
    head_inputs, head_grad = (
        lax.all_to_all(projected, "seq", split_axis=2, concat_axis=0, tiled=True),
        lax.all_to_all(
            local_grad.reshape(tok_count, 1, width_all),
            "seq",
            split_axis=2,
            concat_axis=0,
            tiled=True,
        ),
    )
    head_grad = head_grad.reshape(all_rows, local_cols)
    upper = HD
    result, query_grad, key_grad, value_grad = head_pass(
        head_inputs[:, 0, 0:upper],
        head_inputs[:, 1, 0:upper],
        head_inputs[:, 2, 0:upper],
        head_grad,
        pairs[0, 0],
        valid[0, 0],
    )
    grad_flat = jnp.stack([query_grad, key_grad, value_grad], axis=1).reshape(
        all_rows, 3 * local_cols
    )
    attended = lax.all_to_all(result, "seq", split_axis=0, concat_axis=1, tiled=True)
    local_sum = lax.dot_general(
        lax.all_gather(local_volume, "seq", axis=0, tiled=True),
        grad_flat,
        (((0,), (0,)), ((), ())),
        preferred_element_type=jnp.float32,
    )
    weight_part = (
        lax.psum_scatter(local_sum.astype(jnp.bfloat16), "dp", scatter_dimension=0, tiled=True)
        .astype(jnp.float32)
        .reshape(-1, 3, local_cols)
    )
    return (attended[None], weight_part)


def solution(mesh):
    return jax.shard_map(
        local,
        mesh=mesh,
        in_specs=(
            P("dp", "seq", None),
            P("dp", "seq", None),
            P("dp", None, None),
            P("dp", "seq", None, None),
            P("dp", "seq", None, None),
        ),
        out_specs=(P("dp", "seq", None), P("dp", None, "seq")),
        check_vma=False,
    )
```

profile of v0, /device:TPU:16, one launch (start us, length us, event | category | flops | bytes accessed | tf_op | source)
XLA Modules:
  0.0 509.1 jit_solution(6228003603930186872)
XLA Ops:
  8.7 2.4 copy.66
  11.6 4.1 reduce
  15.7 1.3 reshape.121
  17.1 10.4 %all-to-all-start.1 = ((bf16[16,2,6144]{2,1,0:T(2,128)(2,1)}), bf16[16,2,6144]{2,1,0:T(2,128)(2,1)S(1)}, u32[]{:S(2)}, u32[]{:S(2)}) async-start(bf16[16,2,6144]{2,1,0:T(2,128)(2,1)} %reshape.121), calls=%async_computation.1 | async-start | bytes 786432 | tf_op jit(solution)/shard_map/all_to_all | solution.py:107
  27.5 81.9 %all-gather.4.cloned.1.call-done = bf16[1024,3,1024]{2,0,1:T(8,128)(2,1)} async-done(((bf16[32,3,1024]{2,0,1:T(8,128)(2,1)}), bf16[1024,3,1024]{2,0,1:T(8,128)(2,1)}) %all-gather.4.cloned.1.call-update) | async-done | bytes 6291472 | tf_op jit(solution)/shard_map/all_gather | solution.py:101
  109.4 4.2 convolution_convert_fusion.2
  113.6 2.6 copy.63
  116.2 7.6 %all-to-all-start = ((bf16[192,3,1024]{0,1,2:T(4,128)(2,1)}), bf16[192,3,1024]{0,1,2:T(4,128)(2,1)S(1)}, u32[]{:S(2)}, u32[]{:S(2)}) async-start(bf16[192,3,1024]{0,1,2:T(4,128)(2,1)} %copy.63), calls=%async_computation | async-start | bytes 4194304 | tf_op jit(solution)/shard_map/all_to_all | solution.py:106
  125.4 2.0 reshape.122
  127.4 1.3 copy.95
  129.0 1.4 reshape_reshape.3
  130.4 57.3 %all-to-all-done = bf16[192,3,1024]{0,1,2:T(4,128)(2,1)S(1)} async-done(((bf16[192,3,1024]{0,1,2:T(4,128)(2,1)}), bf16[192,3,1024]{0,1,2:T(4,128)(2,1)S(1)}, u32[]{:S(2)}, u32[]{:S(2)}) %all-to-all-start) | async-done | bytes 1179680 | tf_op jit(solution)/shard_map/all_to_all | solution.py:106
  187.9 0.9 copy.65
  188.8 1.7 all_to_all.39
  190.6 1.2 copy.85
  191.7 1.2 copy.86
  192.9 1.1 reshape_squeeze.20
  194.0 83.2 %while.17 = (s32[]{:T(128)}, f32[24,128,64]{1,0,2:T(8,128)S(1)}, f32[24,128,64]{1,0,2:T(8,128)}, bf16[6,4,128,64]{2,1,0,3:T(4,128)(2,1)}, bf16[6,4,128,64]{2,1,0...) while((s32[]{:T(128)}, f32[24,128,64]{1,0,2:T(8,128)S(1)}, ...), condition=%wide.region_4.5_spmd.clone, body=%wide.region_0.4_spmd.clone.sunk | while | flops 280955456 | bytes 27224828 | solution.py:79
  194.7 1.8 gather_fusion.1
  196.6 0.9 constant_dynamic-slice_fusion.7
  197.9 0.9 fusion.85
  198.9 1.8 gather_fusion
  200.7 0.9 constant_dynamic-slice_fusion.6
  202.7 0.8 copy_dynamic-update-slice_fusion.3
  207.0 0.9 copy-done.1
  208.7 1.8 gather_fusion.1
  210.4 0.9 constant_dynamic-slice_fusion.7
  211.8 0.9 fusion.85
  212.8 1.8 gather_fusion
  214.6 0.9 constant_dynamic-slice_fusion.6
  220.8 0.9 copy-done.1
  222.5 1.8 gather_fusion.1
  224.3 0.9 constant_dynamic-slice_fusion.7
  225.6 0.9 fusion.85
  226.7 1.8 gather_fusion
  228.4 0.9 constant_dynamic-slice_fusion.6
  234.7 0.9 copy-done.1
  236.4 1.8 gather_fusion.1
  238.2 0.9 constant_dynamic-slice_fusion.7
  239.5 0.9 fusion.85
  240.5 1.8 gather_fusion
  242.3 0.9 constant_dynamic-slice_fusion.6
  248.6 0.9 copy-done.1
  250.2 1.8 gather_fusion.1
  252.0 0.9 constant_dynamic-slice_fusion.7
  253.4 0.9 fusion.85
  254.4 1.8 gather_fusion
  256.2 0.9 constant_dynamic-slice_fusion.6
  258.1 0.8 copy_dynamic-update-slice_fusion.3
  262.4 0.9 copy-done.1
  264.1 1.8 gather_fusion.1
  265.9 0.9 constant_dynamic-slice_fusion.7
  267.2 0.9 fusion.85
  268.2 1.8 gather_fusion
  270.0 0.9 constant_dynamic-slice_fusion.6
  272.0 0.8 copy_dynamic-update-slice_fusion.3
  276.3 0.9 copy-done.1
  277.4 0.9 copy-done.2
  279.0 4.2 fusion.34
  283.2 1.0 copy.87
  284.8 23.0 %all_to_all.49 = bf16[16,192,64]{1,2,0:T(8,128)(2,1)S(1)} all-to-all(bf16[16,192,64]{1,2,0:T(8,128)(2,1)S(1)} %copy.75), channel_id=1, replica_groups=mesh['dp'=32,'seq'=16] {'seq'}, dimensions={0} | all-to-all | bytes 786432 | tf_op jit(solution)/shard_map/all_to_all | solution.py:128
  307.8 0.9 copy.77
  308.7 191.4 %reduce-scatter.4.cloned.1.call-done = bf16[32,192]{1,0:T(8,128)(2,1)} async-done(((bf16[1024,192]{1,0:T(8,128)(2,1)}), bf16[32,192]{1,0:T(8,128)(2,1)}) %reduce-scatter.4.cloned.1.call-update) | async-done | bytes 12304
  500.1 0.8 copy.88
  (215 shorter events, 43.2 us)
Async XLA Ops:
  8.0 101.4 %all-gather.4.cloned.1.call-start = ((), (), s32[]{:S(2)}) async-start(), calls=%async_computation.4 | async-start | bytes 6488064 | tf_op jit(solution)/shard_map/all_gather | solution.py:101
  11.6 97.8 %copy-start.3 = (bf16[1,192,1024]{2,1,0:T(8,128)(2,1)S(1)}, bf16[1,192,1024]{2,1,0:T(8,128)(2,1)}, u32[]{:S(2)}) copy-start(bf16[1,192,1024]{2,1,0:T(8,128)(2,1)} %param.7) | copy-start | bytes 1179652
  17.1 99.1 %all-to-all-start.1 = ((bf16[16,2,6144]{2,1,0:T(2,128)(2,1)}), bf16[16,2,6144]{2,1,0:T(2,128)(2,1)S(1)}, u32[]{:S(2)}, u32[]{:S(2)}) async-start(bf16[16,2,6144]{2,1,0:T(2,128)(2,1)} %reshape.121), calls=%async_computation.1 | async-start | bytes 786432 | tf_op jit(solution)/shard_map/all_to_all | solution.py:107
  116.2 8.5 %copy-start.8 = (s32[1,1,24,4]{2,3,1,0:T(4,128)S(1)}, s32[1,1,24,4]{2,3,1,0:T(4,128)}, u32[]{:S(2)}) copy-start(s32[1,1,24,4]{2,3,1,0:T(4,128)} %param.10) | copy-start | bytes 1156
  116.2 9.2 %copy-start.9 = (s32[1,1,24,4]{2,3,1,0:T(4,128)S(1)}, s32[1,1,24,4]{2,3,1,0:T(4,128)}, u32[]{:S(2)}) copy-start(s32[1,1,24,4]{2,3,1,0:T(4,128)} %param.11) | copy-start | bytes 1156
  116.2 71.5 %all-to-all-start = ((bf16[192,3,1024]{0,1,2:T(4,128)(2,1)}), bf16[192,3,1024]{0,1,2:T(4,128)(2,1)S(1)}, u32[]{:S(2)}, u32[]{:S(2)}) async-start(bf16[192,3,1024]{0,1,2:T(4,128)(2,1)} %copy.63), calls=%async_computation | async-start | bytes 4194304 | tf_op jit(solution)/shard_map/all_to_all | solution.py:106
  123.8 155.2 %all-gather.6.cloned.1.call-start = ((), (), s32[]{:S(2)}) async-start(), calls=%async_computation.5 | async-start | bytes 6684672 | tf_op jit(solution)/shard_map/all_gather | solution.py:130
  124.4 375.7 %reduce-scatter.4.cloned.1.call-start = ((), (), s32[]{:S(2)}) async-start(), calls=%async_computation.6 | async-start | bytes 540672
  194.0 4.0 copy-start.6
  203.4 0.9 copy-start.7
  205.1 1.1 copy-start
  207.0 0.9 copy-start.1
  207.9 3.9 copy-start.6
  217.3 0.9 copy-start.7
  219.0 1.1 copy-start
  220.8 0.9 copy-start.1
  221.7 3.9 copy-start.6
  231.2 0.9 copy-start.7
  232.8 1.1 copy-start
  234.7 0.9 copy-start.1
  235.6 3.9 copy-start.6
  245.0 0.9 copy-start.7
  246.7 1.1 copy-start
  248.5 0.9 copy-start.1
  249.4 3.9 copy-start.6
  258.9 0.9 copy-start.7
  260.6 1.1 copy-start
  262.4 0.9 copy-start.1
  263.3 3.9 copy-start.6
  272.7 0.9 copy-start.7
  274.4 1.1 copy-start
  276.3 0.9 copy-start.1
  277.2 1.1 copy-start.2
  277.2 1.3 copy-start.5
  283.2 1.0 copy-start.4
Sparse Core Ops, SparseCore 0:
  12.0 97.3 all-gather.3
  284.4 215.6 reduce-scatter.3
Sparse Core Ops, SparseCore 1:
  126.4 77.8 all-gather.5
where the time goes:
time: 511 us; the launch traced here: 509 us
  waiting for transfers between devices  332 us (65%)
  local copies, waits for them, and re-layouts  76.9 us (15%)
  matrix products  27.8 us (5%)
  blocking collectives  23 us (5%)
  starting transfers between devices  18.3 us (4%)
  between operations  15.7 us (3%)
  other arithmetic  14.6 us (3%)
    unnamed x4, waiting for transfers between devices  193 us
    all_gather x1, waiting for transfers between devices, local(): lax.all_gather(weights, 'dp', axis=0, tiled=True)  81.9 us
    all_to_all x1, waiting for transfers between devices, local(): lax.all_to_all(projected, 'seq', split_axis=2, concat_axis=0, tiled=True)  57.3 us
    all_to_all x1, blocking collectives, local(): lax.all_to_all(result, 'seq', split_axis=0, concat_axis=1, tiled=True)  23 us
    unnamed x24, local copies, waits for them, and re-layouts  12.6 us
    gather x6, local copies, waits for them, and re-layouts, step(): key_blocks[slot_blocks]  10.7 us
    gather x6, local copies, waits for them, and re-layouts, step(): value_blocks[slot_blocks]  10.7 us
    dynamic_slice x12, local copies, waits for them, and re-layouts, head_pass(): lax.scan(step, (empty_acc, empty_acc), sliced_all)  10.5 us
  transfers between devices with their start and end apart: 5, of which 3 were waited for; matrix products, arithmetic and copies ran while one was open for 20% of the time, Pallas kernels for 0%

commit v1 on v0

--- a/solution.py
+++ b/solution.py
@@ -125,7 +125,10 @@
     grad_flat = jnp.stack([query_grad, key_grad, value_grad], axis=1).reshape(
         all_rows, 3 * local_cols
     )
-    attended = lax.all_to_all(result, "seq", split_axis=0, concat_axis=1, tiled=True)
+    attended = jnp.concatenate(
+        lax.all_to_all(jnp.stack(jnp.split(result, lax.axis_size("seq"), axis=0)), "seq", 0, 0),
+        axis=1,
+    )
     local_sum = lax.dot_general(
         lax.all_gather(local_volume, "seq", axis=0, tiled=True),
         grad_flat,

time: 511 us -> 522 us (1.022)
  local copies, waits for them, and re-layouts: 76.9 us -> 87.6 us
    unnamed x24 -> x37, local copies, waits for them, and re-layouts: 12.6 us -> 21.9 us
  transfers between devices with their start and end apart: 5 -> 5, of which waited for: 3 -> 3; matrix products, arithmetic and copies ran while one was open for 20% -> 22% of each run, Pallas kernels for 0% -> 0%
where the time goes in v1:
time: 522 us; the launch traced here: 519 us
  waiting for transfers between devices  331 us (63%)
  local copies, waits for them, and re-layouts  87.6 us (17%)
  matrix products  27.8 us (5%)
  blocking collectives  23.2 us (4%)
  starting transfers between devices  18.3 us (4%)
  between operations  15.7 us (3%)
  other arithmetic  14.6 us (3%)
    unnamed x4, waiting for transfers between devices  192 us
    all_gather x1, waiting for transfers between devices, local(): lax.all_gather(weights, 'dp', axis=0, tiled=True)  81.9 us
    all_to_all x1, waiting for transfers between devices, local(): lax.all_to_all(projected, 'seq', split_axis=2, concat_axis=0, tiled=True)  57.2 us
    all_to_all x1, blocking collectives, local(): lax.all_to_all(jnp.stack(jnp.split(result, lax.axis_size('seq'), axis=0))...  23.2 us
    unnamed x37, local copies, waits for them, and re-layouts  21.9 us
    gather x6, local copies, waits for them, and re-layouts, step(): key_blocks[slot_blocks]  10.7 us
    gather x6, local copies, waits for them, and re-layouts, step(): value_blocks[slot_blocks]  10.7 us
    dynamic_slice x12, local copies, waits for them, and re-layouts, head_pass(): lax.scan(step, (empty_acc, empty_acc), sliced_all)  10.5 us
  transfers between devices with their start and end apart: 5, of which 3 were waited for; matrix products, arithmetic and copies ran while one was open for 22% of the time, Pallas kernels for 0%

profile of v1, /device:TPU:16, one launch (start us, length us, event | category | flops | bytes accessed | tf_op | source)
XLA Modules:
  0.0 519.4 jit_solution(10510475183071606123)
XLA Ops:
  8.7 2.4 copy.79
  11.6 4.1 reduce
  15.7 1.3 reshape.123
  17.1 10.4 %all-to-all-start.1 = ((bf16[16,2,6144]{2,1,0:T(2,128)(2,1)}), bf16[16,2,6144]{2,1,0:T(2,128)(2,1)S(1)}, u32[]{:S(2)}, u32[]{:S(2)}) async-start(bf16[16,2,6144]{2,1,0:T(2,128)(2,1)} %reshape.123), calls=%async_computation.1 | async-start | bytes 786432 | tf_op jit(solution)/shard_map/all_to_all | solution.py:107
  27.5 81.9 %all-gather.4.cloned.1.call-done = bf16[1024,3,1024]{2,0,1:T(8,128)(2,1)} async-done(((bf16[32,3,1024]{2,0,1:T(8,128)(2,1)}), bf16[1024,3,1024]{2,0,1:T(8,128)(2,1)}) %all-gather.4.cloned.1.call-update) | async-done | bytes 6291472 | tf_op jit(solution)/shard_map/all_gather | solution.py:101
  109.4 4.2 convolution_convert_fusion.2
  113.6 2.6 copy.76
  116.2 7.6 %all-to-all-start = ((bf16[192,3,1024]{0,1,2:T(4,128)(2,1)}), bf16[192,3,1024]{0,1,2:T(4,128)(2,1)S(1)}, u32[]{:S(2)}, u32[]{:S(2)}) async-start(bf16[192,3,1024]{0,1,2:T(4,128)(2,1)} %copy.76), calls=%async_computation | async-start | bytes 4194304 | tf_op jit(solution)/shard_map/all_to_all | solution.py:106
  125.4 2.0 reshape.124
  127.4 1.3 copy.107
  129.0 1.4 reshape_reshape.3
  130.4 57.2 %all-to-all-done = bf16[192,3,1024]{0,1,2:T(4,128)(2,1)S(1)} async-done(((bf16[192,3,1024]{0,1,2:T(4,128)(2,1)}), bf16[192,3,1024]{0,1,2:T(4,128)(2,1)S(1)}, u32[]{:S(2)}, u32[]{:S(2)}) %all-to-all-start) | async-done | bytes 1179680 | tf_op jit(solution)/shard_map/all_to_all | solution.py:106
  187.9 0.9 copy.78
  188.8 1.7 all_to_all.30
  190.6 1.2 copy.97
  191.7 1.2 copy.98
  192.9 1.1 reshape_squeeze.20
  194.0 83.1 %while.17 = (s32[]{:T(128)}, f32[24,128,64]{1,0,2:T(8,128)S(1)}, f32[24,128,64]{1,0,2:T(8,128)}, bf16[6,4,128,64]{2,1,0,3:T(4,128)(2,1)}, bf16[6,4,128,64]{2,1,0...) while((s32[]{:T(128)}, f32[24,128,64]{1,0,2:T(8,128)S(1)}, ...), condition=%wide.region_4.5_spmd.clone, body=%wide.region_0.4_spmd.clone.sunk | while | flops 280955456 | bytes 27224828 | solution.py:79
  194.7 1.8 gather_fusion.1
  196.6 0.9 constant_dynamic-slice_fusion.7
  197.9 0.9 fusion.85
  198.9 1.8 gather_fusion
  200.7 0.9 constant_dynamic-slice_fusion.6
  202.7 0.8 copy_dynamic-update-slice_fusion.3
  207.0 0.9 copy-done.1
  208.6 1.8 gather_fusion.1
  210.4 0.9 constant_dynamic-slice_fusion.7
  211.8 0.9 fusion.85
  212.8 1.8 gather_fusion
  214.6 0.9 constant_dynamic-slice_fusion.6
  220.8 0.9 copy-done.1
  222.5 1.8 gather_fusion.1
  224.3 0.9 constant_dynamic-slice_fusion.7
  225.6 0.9 fusion.85
  226.6 1.8 gather_fusion
  228.4 0.9 constant_dynamic-slice_fusion.6
  230.4 0.8 copy_dynamic-update-slice_fusion.3
  234.7 0.9 copy-done.1
  236.3 1.8 gather_fusion.1
  238.1 0.9 constant_dynamic-slice_fusion.7
  239.5 0.9 fusion.85
  240.5 1.8 gather_fusion
  242.3 0.9 constant_dynamic-slice_fusion.6
  244.2 0.8 copy_dynamic-update-slice_fusion.3
  248.5 0.9 copy-done.1
  250.2 1.8 gather_fusion.1
  252.0 0.9 constant_dynamic-slice_fusion.7
  253.3 0.9 fusion.85
  254.3 1.8 gather_fusion
  256.1 0.9 constant_dynamic-slice_fusion.6
  262.4 0.9 copy-done.1
  264.0 1.8 gather_fusion.1
  265.8 0.9 constant_dynamic-slice_fusion.7
  267.2 0.9 fusion.85
  268.2 1.8 gather_fusion
  270.0 0.9 constant_dynamic-slice_fusion.6
  276.2 0.9 copy-done.1
  277.1 1.3 reshape.82
  289.6 4.2 fusion.34
  293.8 1.0 copy.99
  295.5 23.2 %all_to_all.38 = bf16[16,192,64]{1,2,0:T(8,128)(2,1)S(1)} all-to-all(bf16[16,192,64]{1,2,0:T(8,128)(2,1)} %constant_dynamic-update-slice_fusion), channel_id=1, replica_groups=mesh['dp'=32,'seq'=16] {'seq'}, dimensions={0} | all-to-all | bytes 786432 | tf_op jit(solution)/shard_map/all_to_all | solution.py:129
  318.7 0.9 copy.89
  319.6 190.7 %reduce-scatter.4.cloned.1.call-done = bf16[32,192]{1,0:T(8,128)(2,1)} async-done(((bf16[1024,192]{1,0:T(8,128)(2,1)}), bf16[32,192]{1,0:T(8,128)(2,1)}) %reduce-scatter.4.cloned.1.call-update) | async-done | bytes 12304
  510.4 0.8 copy.100
  (228 shorter events, 53.6 us)
Async XLA Ops:
  8.0 101.4 %all-gather.4.cloned.1.call-start = ((), (), s32[]{:S(2)}) async-start(), calls=%async_computation.4 | async-start | bytes 6488064 | tf_op jit(solution)/shard_map/all_gather | solution.py:101
  11.6 97.8 %copy-start.3 = (bf16[1,192,1024]{2,1,0:T(8,128)(2,1)S(1)}, bf16[1,192,1024]{2,1,0:T(8,128)(2,1)}, u32[]{:S(2)}) copy-start(bf16[1,192,1024]{2,1,0:T(8,128)(2,1)} %param.7) | copy-start | bytes 1179652
  17.1 99.1 %all-to-all-start.1 = ((bf16[16,2,6144]{2,1,0:T(2,128)(2,1)}), bf16[16,2,6144]{2,1,0:T(2,128)(2,1)S(1)}, u32[]{:S(2)}, u32[]{:S(2)}) async-start(bf16[16,2,6144]{2,1,0:T(2,128)(2,1)} %reshape.123), calls=%async_computation.1 | async-start | bytes 786432 | tf_op jit(solution)/shard_map/all_to_all | solution.py:107
  116.2 8.5 %copy-start.7 = (s32[1,1,24,4]{2,3,1,0:T(4,128)S(1)}, s32[1,1,24,4]{2,3,1,0:T(4,128)}, u32[]{:S(2)}) copy-start(s32[1,1,24,4]{2,3,1,0:T(4,128)} %param.10) | copy-start | bytes 1156
  116.2 9.2 %copy-start.8 = (s32[1,1,24,4]{2,3,1,0:T(4,128)S(1)}, s32[1,1,24,4]{2,3,1,0:T(4,128)}, u32[]{:S(2)}) copy-start(s32[1,1,24,4]{2,3,1,0:T(4,128)} %param.11) | copy-start | bytes 1156
  116.2 71.5 %all-to-all-start = ((bf16[192,3,1024]{0,1,2:T(4,128)(2,1)}), bf16[192,3,1024]{0,1,2:T(4,128)(2,1)S(1)}, u32[]{:S(2)}, u32[]{:S(2)}) async-start(bf16[192,3,1024]{0,1,2:T(4,128)(2,1)} %copy.76), calls=%async_computation | async-start | bytes 4194304 | tf_op jit(solution)/shard_map/all_to_all | solution.py:106
  123.8 165.8 %all-gather.6.cloned.1.call-start = ((), (), s32[]{:S(2)}) async-start(), calls=%async_computation.5 | async-start | bytes 6684672 | tf_op jit(solution)/shard_map/all_gather | solution.py:133
  124.4 386.0 %reduce-scatter.4.cloned.1.call-start = ((), (), s32[]{:S(2)}) async-start(), calls=%async_computation.6 | async-start | bytes 540672
  194.0 4.0 copy-start.5
  203.4 0.9 copy-start.6
  205.1 1.1 copy-start
  207.0 0.9 copy-start.1
  207.8 3.9 copy-start.5
  217.3 0.9 copy-start.6
  219.0 1.1 copy-start
  220.8 0.9 copy-start.1
  221.7 3.9 copy-start.5
  231.1 0.9 copy-start.6
  232.8 1.1 copy-start
  234.7 0.9 copy-start.1
  235.6 3.9 copy-start.5
  245.0 0.9 copy-start.6
  246.7 1.1 copy-start
  248.5 0.9 copy-start.1
  249.4 3.9 copy-start.5
  258.8 0.9 copy-start.6
  260.5 1.1 copy-start
  262.4 0.9 copy-start.1
  263.3 3.9 copy-start.5
  272.7 0.9 copy-start.6
  274.4 1.1 copy-start
  276.2 0.9 copy-start.1
  277.1 1.6 copy-start.2
  278.5 1.0 copy-start.4
Sparse Core Ops, SparseCore 0:
  12.0 97.3 all-gather.3
  294.9 215.3 reduce-scatter.3
Sparse Core Ops, SparseCore 1:
  126.4 77.8 all-gather.5
